TPU v7x, 768 devices: a whole 4x8x12 slice. The times are simulated.
768 devices in a mesh: tile: 192 (over y_lo, z, x), col: 4 (over y_hi, core).
Axes of the slice: x: 4, y: 8 (y_hi: 2, y_lo: 4; y = y_hi * 4 + y_lo), z: 12, core: 2. Of those that a mesh axis runs over, the one named last changes fastest.
Arguments:
- tracer_old: float32 [192, 6, 128, 128], P('tile', None, 'col'), may hold values from -6 to 6
- u_face: float32 [192, 6, 128, 128], P('tile', None, 'col'), may hold values from -4 to 4
- v_face: float32 [192, 6, 128, 128], P('tile', None, 'col'), may hold values from -4 to 4
- depth_levels: int32 [192, 128, 128], P('tile', 'col'), may hold values from 0 to 6
- cotangent: float32 [192, 6, 128, 128], P('tile', None, 'col'), may hold values from -90 to 90
- surface_diag: float32 [192, 128, 128], P('tile', 'col'), may hold values from 0.2 to 8
- seam_flip: int32 [192], replicated, may hold values from 0 to 1
- step_index: int32 [1], replicated, may hold values from 0 to 23
Outputs:
- adj_tracer: float32 [192, 6, 128, 128], P('tile', None, 'col')
- adj_pressure: float32 [192, 128, 128], P('tile', 'col')
All inputs are finite; a program needn't handle non-finite values.
Results may differ from a plain program's by a relative error of at most 0.0009.
Values sent between devices are 32-bit elements; how exact they have to be, the bound alone decides.
A program may use at most 32 MiB of HBM per device.

v0:
```python
import math

import jax
import jax.numpy as jnp
from jax import lax
from jax.sharding import PartitionSpec as P

ITERS = 2


flux_dt = 0.2
kappa_h = 0.4
kappa_base = 0.1
kappa_conv = 1.0
mix_dt = 0.3
relax_mean = 0.5
relax_swing = 0.8
day_steps = 24.0


def padded(block, sides, width, periodic):
    for axis, dim in sides:
        count = lax.axis_size(axis)
        forward = [(i, i + 1) for i in range(count - 1)]
        if periodic:
            forward.append((count - 1, 0))
        backward = [(target, source) for source, target in forward]
        low = lax.ppermute(
            lax.slice_in_dim(block, block.shape[dim] - width, None, axis=dim), axis, forward
        )
        high = lax.ppermute(lax.slice_in_dim(block, 0, width, axis=dim), axis, backward)
        block = jnp.concatenate([low, block, high], axis=dim)
    return block


def partner(value, axis, apart):
    mask = 2**apart
    pairs = [(source, source ^ mask) for source in range(lax.axis_size(axis))]
    return lax.ppermute(value, axis, pairs)


def wet_levels(depth_float, level_count):
    level_ids = lax.broadcasted_iota(jnp.float32, (level_count,) + depth_float.shape, 0)
    return jnp.where(level_ids < depth_float[None], 1.0, 0.0).astype(jnp.float32)


def flux_divergence(tracer_ext, speed_ext, wet_ext, axis_num, cells):

    def window(values, offset):
        return lax.slice_in_dim(values, offset, offset + cells + 1, axis=axis_num)

    behind = window(tracer_ext, 0)
    center = window(tracer_ext, 1)
    front_cell = window(tracer_ext, 2)
    beyond = window(tracer_ext, 3)
    speeds = window(speed_ext, 1)
    open_face = window(wet_ext, 1) * window(wet_ext, 2)
    face_flux = open_face * (
        speeds * (7.0 * (center + front_cell) - (behind + beyond)) / 12.0
        - kappa_h * (front_cell - center)
    )
    return lax.slice_in_dim(face_flux, 1, cells + 1, axis=axis_num) - lax.slice_in_dim(
        face_flux, 0, cells, axis=axis_num
    )


def flux_adjoint(weight_ext, speed_ext, wet_ext, axis_num, cells):

    def window(values, offset, length):
        return lax.slice_in_dim(values, offset, offset + length, axis=axis_num)

    face_grad = flux_dt * (window(weight_ext, 1, cells + 3) - window(weight_ext, 0, cells + 3))
    open_face = window(wet_ext, 0, cells + 3) * window(wet_ext, 1, cells + 3)
    scaled = face_grad * open_face
    carried = window(speed_ext, 0, cells + 3) * scaled
    summed = -window(carried, 3, cells) / 12.0
    summed = summed + 7.0 * window(carried, 2, cells) / 12.0 + kappa_h * window(scaled, 2, cells)
    summed = summed + 7.0 * window(carried, 1, cells) / 12.0 - kappa_h * window(scaled, 1, cells)
    return summed - window(carried, 0, cells) / 12.0


def vertical_mix(column_state, wet_cells, relax_rate):
    upper_cells = column_state[:-1]
    lower_cells = column_state[1:]
    mix_coef = wet_cells[1:] * (
        kappa_base + kappa_conv * jax.nn.sigmoid(4.0 * (lower_cells - upper_cells))
    )
    face_flux = mix_coef * (upper_cells - lower_cells)
    boundary = jnp.zeros_like(column_state[:1])
    change = jnp.concatenate([face_flux, boundary]) - jnp.concatenate([boundary, face_flux])
    updated = column_state - mix_dt * change
    updated = jnp.concatenate([updated[:1] - relax_rate * column_state[:1], updated[1:]])
    return wet_cells * updated


def cotangent_after_mix(
    masked, masked_x, masked_y, u_x, v_y, wet_cells, wet_x, wet_y, weight_new, relax_rate
):
    level_count, row_count, col_count = masked.shape
    change = flux_divergence(masked_x, u_x, wet_x, 2, col_count) + flux_divergence(
        masked_y, v_y, wet_y, 1, row_count
    )
    mixed = wet_cells * (masked - flux_dt * change)
    _, pullback = jax.vjp(
        lambda column_state: vertical_mix(column_state, wet_cells, relax_rate), mixed
    )
    return wet_cells * pullback(weight_new)[0]


def tracer_adjoint(weight_raw, raw_x, raw_y, u_x, v_y, wet_cells, wet_x, wet_y):
    level_count, row_count, col_count = weight_raw.shape
    summed = (
        weight_raw
        + flux_adjoint(raw_x, u_x, wet_x, 2, col_count)
        + flux_adjoint(raw_y, v_y, wet_y, 1, row_count)
    )
    return wet_cells * summed


def seam_halo(edge_sets):
    return padded(edge_sets, (("tile", 0),), 1, True)


def mirror_rows(pieces):
    mirrored = pieces
    for bit_index in range(lax.axis_size("col").bit_length() - 1):
        mirrored = partner(mirrored, "col", bit_index)
    return mirrored


def below_above(planes, halo_width):
    return padded(planes, (("col", 1),), halo_width, False)


def across_seams(planes, halo_width, seam_flips):
    flip_west, flip_east = seam_flips
    col_count = planes.shape[2]
    pieces = jnp.stack(
        [planes[:, :, :halo_width], planes[:, :, col_count - halo_width :]]
    ).swapaxes(2, 3)
    received = seam_halo(pieces)
    own_side = jnp.stack([received[0], received[3]])
    mirrored = mirror_rows(own_side)
    from_west = jnp.where(flip_west, mirrored[0][..., ::-1], own_side[0])
    from_east = jnp.where(flip_east, mirrored[1][..., ::-1], own_side[1])
    return jnp.concatenate([from_west.swapaxes(1, 2), planes, from_east.swapaxes(1, 2)], axis=2)


def global_total(summand):
    return lax.psum(summand, ("tile", "col"))


def shards(
    tracer_old, u_face, v_face, depth_levels, cotangent, surface_diag, seam_flip, step_index
):
    old_tile = tracer_old[0]
    u_tile = u_face[0]
    v_tile = v_face[0]
    diagonal = surface_diag[0]
    depth_float = depth_levels[0].astype(jnp.float32)
    level_count, row_count, col_count = old_tile.shape
    tile_count = lax.axis_size("tile")
    tile_index = lax.axis_index("tile")
    flip_east = lax.dynamic_slice_in_dim(seam_flip, tile_index, 1)[0] == 1
    flip_west = (
        lax.dynamic_slice_in_dim(seam_flip, (tile_index + tile_count - 1) % tile_count, 1)[0] == 1
    )
    seam_flips = (flip_west, flip_east)
    relax_rate = relax_mean * (
        1.0 + relax_swing * jnp.cos(2.0 * math.pi * step_index[0].astype(jnp.float32) / day_steps)
    )
    wet_cells = wet_levels(depth_float, level_count)
    masked = old_tile * wet_cells
    x_planes = across_seams(
        jnp.concatenate([masked, u_tile, depth_float[None]], axis=0), 2, seam_flips
    )
    y_planes = below_above(jnp.concatenate([masked, v_tile, depth_float[None]], axis=0), 2)
    masked_x = x_planes[:level_count]
    u_x = x_planes[level_count : 2 * level_count]
    wet_x = wet_levels(x_planes[2 * level_count], level_count)
    masked_y = y_planes[:level_count]
    v_y = y_planes[level_count : 2 * level_count]
    wet_y = wet_levels(y_planes[2 * level_count], level_count)
    weight_raw = cotangent_after_mix(
        masked, masked_x, masked_y, u_x, v_y, wet_cells, wet_x, wet_y, cotangent[0], relax_rate
    )
    raw_x = across_seams(weight_raw, 2, seam_flips)
    raw_y = below_above(weight_raw, 2)
    adjoint_tile = tracer_adjoint(weight_raw, raw_x, raw_y, u_x, v_y, wet_cells, wet_x, wet_y)
    rhs = jnp.sum(adjoint_tile, axis=0)
    wet_top = wet_cells[0]
    east_open = wet_top * wet_x[0][:, 3 : col_count + 3]
    west_open = wet_top * wet_x[0][:, 1 : col_count + 1]
    north_open = wet_top * wet_y[0][3 : row_count + 3]
    south_open = wet_top * wet_y[0][1 : row_count + 1]
    solution = jnp.zeros_like(rhs)
    residual = rhs
    direction = rhs
    norm_now = global_total(jnp.sum(residual * residual))
    for iteration in range(ITERS):
        side_vals = across_seams(direction[None], 1, seam_flips)[0]
        row_vals = below_above(direction[None], 1)[0]
        east_vals = side_vals[:, 2:]
        west_vals = side_vals[:, :col_count]
        north_vals = row_vals[2:]
        south_vals = row_vals[:row_count]
        applied = (
            diagonal * direction
            + east_open * (direction - east_vals)
            + west_open * (direction - west_vals)
        )
        applied = (
            applied + north_open * (direction - north_vals) + south_open * (direction - south_vals)
        )
        step_size = norm_now / global_total(jnp.sum(direction * applied))
        solution = solution + step_size * direction
        if iteration + 1 < ITERS:
            residual = residual - step_size * applied
            norm_next = global_total(jnp.sum(residual * residual))
            direction = residual + norm_next / norm_now * direction
            norm_now = norm_next
    return (adjoint_tile[None], solution[None])


def solution(mesh):
    in_specs = (
        P("tile", None, "col", None),
        P("tile", None, "col", None),
        P("tile", None, "col", None),
        P("tile", "col", None),
        P("tile", None, "col", None),
        P("tile", "col", None),
        P(),
        P(),
    )
    out_specs = (P("tile", None, "col", None), P("tile", "col", None))
    return jax.shard_map(shards, mesh=mesh, in_specs=in_specs, out_specs=out_specs, check_vma=False)
```

profile of v0, /device:TPU:1, one launch (start us, length us, event | category | flops | bytes accessed | tf_op | source)
XLA Modules:
  0.0 484.1 jit_solution(1281557082859876271)
XLA Ops:
  0.6 0.7 convert_bitcast_fusion
  1.4 1.0 fusion.37
  2.4 0.1 slice_bitcast_fusion.1
  2.6 0.1 copy.52
  2.7 0.2 copy.53
  2.9 3.9 collective-permute-start
  6.9 18.3 %collective-permute-start.1 = (f32[1,13,2,32]{3,2,1,0:T(2,128)S(1)}, f32[1,13,2,32]{3,2,1,0:T(2,128)S(1)}, u32[]{:S(2)}, u32[]{:S(2)}) collective-permute-start(f32[1,13,2,32]{3,2,1,0:T(2,128)S(1)} %get-tuple-element.35), channel_id=1, source_target_pairs={{4,0},{8,4},{12,8},{16,12},{20,16},{24,20},{28,24},{32,28},{36,32}... | collective-permute-start | bytes 9992 | tf_op jit(solution)/shard_map/ppermute | solution.py:31
  25.2 5.6 %collective-permute-start.4 = (f32[13,2,128]{2,1,0:T(2,128)S(1)}, f32[13,2,128]{2,1,0:T(2,128)S(1)}, u32[]{:S(2)}, u32[]{:S(2)}) collective-permute-start(f32[13,2,128]{2,1,0:T(2,128)S(1)} %get-tuple-element.24), channel_id=1, source_target_pairs={{0,1},{1,2},{2,3},{4,5},{5,6},{6,7},{8,9},{9,10},{10,11},{12,13},{... | collective-permute-start | bytes 39944 | tf_op jit(solution)/shard_map/ppermute | solution.py:28
  30.8 1.9 collective-permute-start.5
  32.8 0.6 copy-done.4
  34.3 1.9 collective-permute-start.2
  36.3 0.7 copy-done.5
  36.9 0.6 fusion.89
  38.8 7.7 %collective-permute-start.3 = (f32[2,13,2,32]{3,2,1,0:T(2,128)S(1)}, f32[2,13,2,32]{3,2,1,0:T(2,128)S(1)}, u32[]{:S(2)}, u32[]{:S(2)}) collective-permute-start(f32[2,13,2,32]{3,2,1,0:T(2,128)S(1)} %collective-permute-done.2), channel_id=1, source_target_pairs={{0,2},{1,3},{2,0},{3,1},{4,6},{5,7},{6,4},{7,5},{8,10},{9,11},{10,... | collective-permute-start | bytes 19976 | tf_op jit(solution)/shard_map/ppermute | solution.py:39
  46.7 1.0 collective-permute-done.3
  47.7 0.1 rev.24
  47.8 0.2 copy.54
  48.0 0.1 rev.25
  48.1 0.2 copy.55
  48.3 0.2 maximum_maximum_fusion
  48.6 0.3 fusion.8
  48.9 0.5 copy-done.2
  50.0 0.1 copy.59
  50.1 1.9 collective-permute-start.6
  52.0 9.4 %collective-permute-start.7 = (f32[1,6,2,32]{3,2,1,0:T(2,128)S(1)}, f32[1,6,2,32]{3,2,1,0:T(2,128)S(1)}, u32[]{:S(2)}, u32[]{:S(2)}) collective-permute-start(f32[1,6,2,32]{3,2,1,0:T(2,128)S(1)} %get-tuple-element.48), channel_id=1, source_target_pairs={{4,0},{8,4},{12,8},{16,12},{20,16},{24,20},{28,24},{32,28},{36,32}... | collective-permute-start | bytes 4616 | tf_op jit(solution)/shard_map/ppermute | solution.py:31
  61.4 8.9 %collective-permute-start.10 = (f32[6,2,128]{2,1,0:T(2,128)S(1)}, f32[6,2,128]{2,1,0:T(2,128)S(1)}, u32[]{:S(2)}, u32[]{:S(2)}) collective-permute-start(f32[6,2,128]{2,1,0:T(2,128)S(1)} %get-tuple-element.30), channel_id=1, source_target_pairs={{0,1},{1,2},{2,3},{4,5},{5,6},{6,7},{8,9},{9,10},{10,11},{12,13},{... | collective-permute-start | bytes 18440 | tf_op jit(solution)/shard_map/ppermute | solution.py:28
  70.3 1.9 collective-permute-start.11
  72.3 1.9 collective-permute-start.8
  74.2 1.1 collective-permute-done.8
  75.4 7.3 %collective-permute-start.9 = (f32[2,6,2,32]{3,2,1,0:T(2,128)S(1)}, f32[2,6,2,32]{3,2,1,0:T(2,128)S(1)}, u32[]{:S(2)}, u32[]{:S(2)}) collective-permute-start(f32[2,6,2,32]{3,2,1,0:T(2,128)S(1)} %collective-permute-done.8), channel_id=1, source_target_pairs={{0,2},{1,3},{2,0},{3,1},{4,6},{5,7},{6,4},{7,5},{8,10},{9,11},{10,... | collective-permute-start | bytes 9224 | tf_op jit(solution)/shard_map/ppermute | solution.py:39
  82.8 1.0 collective-permute-done.9
  83.9 0.1 copy.60
  84.1 0.1 copy.61
  84.2 0.1 pad_maximum_fusion.12
  84.4 0.3 fusion.2
  84.6 0.9 fusion.79
  85.5 0.2 slice_reduce_fusion.3
  85.6 1.9 collective-permute-start.12
  87.6 9.4 %collective-permute-start.13 = (f32[1,1,1,32]{3,2,1,0:T(1,128)S(1)}, f32[1,1,1,32]{3,2,1,0:T(1,128)S(1)}, u32[]{:S(2)}, u32[]{:S(2)}) collective-permute-start(f32[1,1,1,32]{3,2,1,0:T(1,128)S(1)} %bitcast.211), channel_id=1, source_target_pairs={{4,0},{8,4},{12,8},{16,12},{20,16},{24,20},{28,24},{32,28},{36,32}... | collective-permute-start | bytes 392 | tf_op jit(solution)/shard_map/ppermute | solution.py:31
  97.0 0.7 collective-permute-done.13
  97.7 4.3 collective-permute-start.14
  102.0 0.8 collective-permute-done.14
  102.8 7.5 %collective-permute-start.15 = (f32[2,1,1,32]{3,2,1,0:T(1,128)S(1)}, f32[2,1,1,32]{3,2,1,0:T(1,128)S(1)}, u32[]{:S(2)}, u32[]{:S(2)}) collective-permute-start(f32[2,1,1,32]{3,2,1,0:T(1,128)S(1)} %collective-permute-done.14), channel_id=1, source_target_pairs={{0,2},{1,3},{2,0},{3,1},{4,6},{5,7},{6,4},{7,5},{8,10},{9,11},{10,... | collective-permute-start | bytes 776 | tf_op jit(solution)/shard_map/ppermute | solution.py:39
  110.3 2.5 collective-permute-start.16
  112.8 7.0 %collective-permute-start.17 = (f32[1,1,128]{2,1,0:T(1,128)S(1)}, f32[1,1,128]{2,1,0:T(1,128)S(1)}, u32[]{:S(2)}, u32[]{:S(2)}) collective-permute-start(f32[1,1,128]{2,1,0:T(1,128)S(1)} %get-tuple-element.39), channel_id=1, source_target_pairs={{0,1},{1,2},{2,3},{4,5},{5,6},{6,7},{8,9},{9,10},{10,11},{12,13},{... | collective-permute-start | bytes 1544 | tf_op jit(solution)/shard_map/ppermute | solution.py:28
  120.3 0.2 collective-permute-done.17
  120.5 0.4 copy-done.3
  120.9 0.7 multiply_reduce_fusion.1
  121.6 109.5 %all-reduce.4 = (f32[]{:T(128)}, f32[]{:T(128)}) all-reduce(f32[]{:T(128)} %get-tuple-element.7, f32[]{:T(128)} %get-tuple-element.6), channel_id=1, replica_groups=mesh['tile'=192,'col'=4] {'tile','col'}, use_global_device_ids=true, to_apply=%region_2.3 | all-reduce | flops 2 | bytes 16 | tf_op jit(solution)/shard_map/psum | solution.py:150
  232.5 0.6 multiply_reduce_fusion
  233.1 103.7 %psum.30 = f32[]{:T(128)} all-reduce(f32[]{:T(128)} %multiply_reduce_fusion), channel_id=1, replica_groups=mesh['tile'=192,'col'=4] {'tile','col'}, use_global_device_ids=true, to_apply=%region_6.7 | all-reduce | flops 1 | bytes 8 | tf_op jit(solution)/shard_map/psum | solution.py:150
  338.1 0.2 slice_reduce_fusion.1
  338.2 3.7 collective-permute-start.18
  341.9 7.6 %collective-permute-start.19 = (f32[1,1,1,32]{3,2,1,0:T(1,128)S(1)}, f32[1,1,1,32]{3,2,1,0:T(1,128)S(1)}, u32[]{:S(2)}, u32[]{:S(2)}) collective-permute-start(f32[1,1,1,32]{3,2,1,0:T(1,128)S(1)} %bitcast.212), channel_id=1, source_target_pairs={{4,0},{8,4},{12,8},{16,12},{20,16},{24,20},{28,24},{32,28},{36,32}... | collective-permute-start | bytes 392 | tf_op jit(solution)/shard_map/ppermute | solution.py:31
  349.6 0.7 collective-permute-done.19
  350.3 3.7 collective-permute-start.20
  354.0 0.8 collective-permute-done.20
  354.8 6.7 %collective-permute-start.21 = (f32[2,1,1,32]{3,2,1,0:T(1,128)S(1)}, f32[2,1,1,32]{3,2,1,0:T(1,128)S(1)}, u32[]{:S(2)}, u32[]{:S(2)}) collective-permute-start(f32[2,1,1,32]{3,2,1,0:T(1,128)S(1)} %collective-permute-done.20), channel_id=1, source_target_pairs={{0,2},{1,3},{2,0},{3,1},{4,6},{5,7},{6,4},{7,5},{8,10},{9,11},{10,... | collective-permute-start | bytes 776 | tf_op jit(solution)/shard_map/ppermute | solution.py:39
  361.4 2.5 collective-permute-start.22
  364.0 7.0 %collective-permute-start.23 = (f32[1,1,128]{2,1,0:T(1,128)S(1)}, f32[1,1,128]{2,1,0:T(1,128)S(1)}, u32[]{:S(2)}, u32[]{:S(2)}) collective-permute-start(f32[1,1,128]{2,1,0:T(1,128)S(1)} %get-tuple-element.37), channel_id=1, source_target_pairs={{0,1},{1,2},{2,3},{4,5},{5,6},{6,7},{8,9},{9,10},{10,11},{12,13},{... | collective-permute-start | bytes 1544 | tf_op jit(solution)/shard_map/ppermute | solution.py:28
  371.4 0.2 collective-permute-done.23
  371.6 0.7 fusion.45
  372.3 109.9 %psum.31 = f32[]{:T(128)} all-reduce(f32[]{:T(128)} %fusion.45), channel_id=1, replica_groups=mesh['tile'=192,'col'=4] {'tile','col'}, use_global_device_ids=true, to_apply=%region_8.9 | all-reduce | flops 1 | bytes 8 | tf_op jit(solution)/shard_map/psum | solution.py:150
  483.5 0.6 add_bitcast_fusion
  (79 shorter events, 2.3 us)
Async XLA Ops:
  1.4 1.0 copy-start
  1.4 1.0 copy-start.1
  2.9 31.3 %collective-permute-start = (f32[1,13,2,32]{3,2,1,0:T(2,128)S(1)}, f32[1,13,2,32]{3,2,1,0:T(2,128)S(1)}, u32[]{:S(2)}, u32[]{:S(2)}) collective-permute-start(f32[1,13,2,32]{3,2,1,0:T(2,128)S(1)} %get-tuple-element.34), channel_id=1, source_target_pairs={{0,4},{4,8},{8,12},{12,16},{16,20},{20,24},{24,28},{28,32},{32,36}... | collective-permute-start | bytes 9992 | tf_op jit(solution)/shard_map/ppermute | solution.py:28
  6.9 27.4 %collective-permute-start.1 = (f32[1,13,2,32]{3,2,1,0:T(2,128)S(1)}, f32[1,13,2,32]{3,2,1,0:T(2,128)S(1)}, u32[]{:S(2)}, u32[]{:S(2)}) collective-permute-start(f32[1,13,2,32]{3,2,1,0:T(2,128)S(1)} %get-tuple-element.35), channel_id=1, source_target_pairs={{4,0},{8,4},{12,8},{16,12},{20,16},{24,20},{28,24},{32,28},{36,32}... | collective-permute-start | bytes 9992 | tf_op jit(solution)/shard_map/ppermute | solution.py:31
  25.2 21.3 %collective-permute-start.4 = (f32[13,2,128]{2,1,0:T(2,128)S(1)}, f32[13,2,128]{2,1,0:T(2,128)S(1)}, u32[]{:S(2)}, u32[]{:S(2)}) collective-permute-start(f32[13,2,128]{2,1,0:T(2,128)S(1)} %get-tuple-element.24), channel_id=1, source_target_pairs={{0,1},{1,2},{2,3},{4,5},{5,6},{6,7},{8,9},{9,10},{10,11},{12,13},{... | collective-permute-start | bytes 39944 | tf_op jit(solution)/shard_map/ppermute | solution.py:28
  30.8 15.7 %collective-permute-start.5 = (f32[13,2,128]{2,1,0:T(2,128)S(1)}, f32[13,2,128]{2,1,0:T(2,128)S(1)}, u32[]{:S(2)}, u32[]{:S(2)}) collective-permute-start(f32[13,2,128]{2,1,0:T(2,128)S(1)} %get-tuple-element.25), channel_id=1, source_target_pairs={{1,0},{2,1},{3,2},{5,4},{6,5},{7,6},{9,8},{10,9},{11,10},{13,12},{... | collective-permute-start | bytes 39944 | tf_op jit(solution)/shard_map/ppermute | solution.py:31
  32.8 0.7 copy-start.4
  34.3 4.5 collective-permute-start.2
  36.3 0.7 copy-start.5
  38.8 8.9 %collective-permute-start.3 = (f32[2,13,2,32]{3,2,1,0:T(2,128)S(1)}, f32[2,13,2,32]{3,2,1,0:T(2,128)S(1)}, u32[]{:S(2)}, u32[]{:S(2)}) collective-permute-start(f32[2,13,2,32]{3,2,1,0:T(2,128)S(1)} %collective-permute-done.2), channel_id=1, source_target_pairs={{0,2},{1,3},{2,0},{3,1},{4,6},{5,7},{6,4},{7,5},{8,10},{9,11},{10,... | collective-permute-start | bytes 19976 | tf_op jit(solution)/shard_map/ppermute | solution.py:39
  48.6 0.9 copy-start.2
  50.1 22.1 %collective-permute-start.6 = (f32[1,6,2,32]{3,2,1,0:T(2,128)S(1)}, f32[1,6,2,32]{3,2,1,0:T(2,128)S(1)}, u32[]{:S(2)}, u32[]{:S(2)}) collective-permute-start(f32[1,6,2,32]{3,2,1,0:T(2,128)S(1)} %get-tuple-element.47), channel_id=1, source_target_pairs={{0,4},{4,8},{8,12},{12,16},{16,20},{20,24},{24,28},{28,32},{32,36}... | collective-permute-start | bytes 4616 | tf_op jit(solution)/shard_map/ppermute | solution.py:28
  52.0 20.2 %collective-permute-start.7 = (f32[1,6,2,32]{3,2,1,0:T(2,128)S(1)}, f32[1,6,2,32]{3,2,1,0:T(2,128)S(1)}, u32[]{:S(2)}, u32[]{:S(2)}) collective-permute-start(f32[1,6,2,32]{3,2,1,0:T(2,128)S(1)} %get-tuple-element.48), channel_id=1, source_target_pairs={{4,0},{8,4},{12,8},{16,12},{20,16},{24,20},{28,24},{32,28},{36,32}... | collective-permute-start | bytes 4616 | tf_op jit(solution)/shard_map/ppermute | solution.py:31
  61.4 21.2 %collective-permute-start.10 = (f32[6,2,128]{2,1,0:T(2,128)S(1)}, f32[6,2,128]{2,1,0:T(2,128)S(1)}, u32[]{:S(2)}, u32[]{:S(2)}) collective-permute-start(f32[6,2,128]{2,1,0:T(2,128)S(1)} %get-tuple-element.30), channel_id=1, source_target_pairs={{0,1},{1,2},{2,3},{4,5},{5,6},{6,7},{8,9},{9,10},{10,11},{12,13},{... | collective-permute-start | bytes 18440 | tf_op jit(solution)/shard_map/ppermute | solution.py:28
  70.3 12.4 %collective-permute-start.11 = (f32[6,2,128]{2,1,0:T(2,128)S(1)}, f32[6,2,128]{2,1,0:T(2,128)S(1)}, u32[]{:S(2)}, u32[]{:S(2)}) collective-permute-start(f32[6,2,128]{2,1,0:T(2,128)S(1)} %get-tuple-element.31), channel_id=1, source_target_pairs={{1,0},{2,1},{3,2},{5,4},{6,5},{7,6},{9,8},{10,9},{11,10},{13,12},{... | collective-permute-start | bytes 18440 | tf_op jit(solution)/shard_map/ppermute | solution.py:31
  72.3 3.1 collective-permute-start.8
  75.4 8.4 %collective-permute-start.9 = (f32[2,6,2,32]{3,2,1,0:T(2,128)S(1)}, f32[2,6,2,32]{3,2,1,0:T(2,128)S(1)}, u32[]{:S(2)}, u32[]{:S(2)}) collective-permute-start(f32[2,6,2,32]{3,2,1,0:T(2,128)S(1)} %collective-permute-done.8), channel_id=1, source_target_pairs={{0,2},{1,3},{2,0},{3,1},{4,6},{5,7},{6,4},{7,5},{8,10},{9,11},{10,... | collective-permute-start | bytes 9224 | tf_op jit(solution)/shard_map/ppermute | solution.py:39
  85.6 11.3 %collective-permute-start.12 = (f32[1,1,1,32]{3,2,1,0:T(1,128)S(1)}, f32[1,1,1,32]{3,2,1,0:T(1,128)S(1)}, u32[]{:S(2)}, u32[]{:S(2)}) collective-permute-start(f32[1,1,1,32]{3,2,1,0:T(1,128)S(1)} %bitcast.213), channel_id=1, source_target_pairs={{0,4},{4,8},{8,12},{12,16},{16,20},{20,24},{24,28},{28,32},{32,36}... | collective-permute-start | bytes 392 | tf_op jit(solution)/shard_map/ppermute | solution.py:28
  87.6 10.1 %collective-permute-start.13 = (f32[1,1,1,32]{3,2,1,0:T(1,128)S(1)}, f32[1,1,1,32]{3,2,1,0:T(1,128)S(1)}, u32[]{:S(2)}, u32[]{:S(2)}) collective-permute-start(f32[1,1,1,32]{3,2,1,0:T(1,128)S(1)} %bitcast.211), channel_id=1, source_target_pairs={{4,0},{8,4},{12,8},{16,12},{20,16},{24,20},{28,24},{32,28},{36,32}... | collective-permute-start | bytes 392 | tf_op jit(solution)/shard_map/ppermute | solution.py:31
  97.7 5.1 %collective-permute-start.14 = (f32[2,1,1,32]{3,2,1,0:T(1,128)S(1)}, f32[2,1,1,32]{3,2,1,0:T(1,128)S(1)}, u32[]{:S(2)}, u32[]{:S(2)}) collective-permute-start(f32[2,1,1,32]{3,2,1,0:T(1,128)S(1)} %pad_maximum_fusion.28), channel_id=1, source_target_pairs={{0,1},{1,0},{2,3},{3,2},{4,5},{5,4},{6,7},{7,6},{8,9},{9,8},{10,11... | collective-permute-start | bytes 776 | tf_op jit(solution)/shard_map/ppermute | solution.py:39
  102.8 17.0 %collective-permute-start.15 = (f32[2,1,1,32]{3,2,1,0:T(1,128)S(1)}, f32[2,1,1,32]{3,2,1,0:T(1,128)S(1)}, u32[]{:S(2)}, u32[]{:S(2)}) collective-permute-start(f32[2,1,1,32]{3,2,1,0:T(1,128)S(1)} %collective-permute-done.14), channel_id=1, source_target_pairs={{0,2},{1,3},{2,0},{3,1},{4,6},{5,7},{6,4},{7,5},{8,10},{9,11},{10,... | collective-permute-start | bytes 776 | tf_op jit(solution)/shard_map/ppermute | solution.py:39
  110.3 10.0 %collective-permute-start.16 = (f32[1,1,128]{2,1,0:T(1,128)S(1)}, f32[1,1,128]{2,1,0:T(1,128)S(1)}, u32[]{:S(2)}, u32[]{:S(2)}) collective-permute-start(f32[1,1,128]{2,1,0:T(1,128)S(1)} %get-tuple-element.38), channel_id=1, source_target_pairs={{1,0},{2,1},{3,2},{5,4},{6,5},{7,6},{9,8},{10,9},{11,10},{13,12},{... | collective-permute-start | bytes 1544 | tf_op jit(solution)/shard_map/ppermute | solution.py:31
  112.8 7.7 %collective-permute-start.17 = (f32[1,1,128]{2,1,0:T(1,128)S(1)}, f32[1,1,128]{2,1,0:T(1,128)S(1)}, u32[]{:S(2)}, u32[]{:S(2)}) collective-permute-start(f32[1,1,128]{2,1,0:T(1,128)S(1)} %get-tuple-element.39), channel_id=1, source_target_pairs={{0,1},{1,2},{2,3},{4,5},{5,6},{6,7},{8,9},{9,10},{10,11},{12,13},{... | collective-permute-start | bytes 1544 | tf_op jit(solution)/shard_map/ppermute | solution.py:28
  120.2 0.7 copy-start.3
  338.2 11.3 %collective-permute-start.18 = (f32[1,1,1,32]{3,2,1,0:T(1,128)S(1)}, f32[1,1,1,32]{3,2,1,0:T(1,128)S(1)}, u32[]{:S(2)}, u32[]{:S(2)}) collective-permute-start(f32[1,1,1,32]{3,2,1,0:T(1,128)S(1)} %bitcast.214), channel_id=1, source_target_pairs={{0,4},{4,8},{8,12},{12,16},{16,20},{20,24},{24,28},{28,32},{32,36}... | collective-permute-start | bytes 392 | tf_op jit(solution)/shard_map/ppermute | solution.py:28
  341.9 8.4 %collective-permute-start.19 = (f32[1,1,1,32]{3,2,1,0:T(1,128)S(1)}, f32[1,1,1,32]{3,2,1,0:T(1,128)S(1)}, u32[]{:S(2)}, u32[]{:S(2)}) collective-permute-start(f32[1,1,1,32]{3,2,1,0:T(1,128)S(1)} %bitcast.212), channel_id=1, source_target_pairs={{4,0},{8,4},{12,8},{16,12},{20,16},{24,20},{28,24},{32,28},{36,32}... | collective-permute-start | bytes 392 | tf_op jit(solution)/shard_map/ppermute | solution.py:31
  350.3 4.5 collective-permute-start.20
  354.8 16.2 %collective-permute-start.21 = (f32[2,1,1,32]{3,2,1,0:T(1,128)S(1)}, f32[2,1,1,32]{3,2,1,0:T(1,128)S(1)}, u32[]{:S(2)}, u32[]{:S(2)}) collective-permute-start(f32[2,1,1,32]{3,2,1,0:T(1,128)S(1)} %collective-permute-done.20), channel_id=1, source_target_pairs={{0,2},{1,3},{2,0},{3,1},{4,6},{5,7},{6,4},{7,5},{8,10},{9,11},{10,... | collective-permute-start | bytes 776 | tf_op jit(solution)/shard_map/ppermute | solution.py:39
  361.4 10.0 %collective-permute-start.22 = (f32[1,1,128]{2,1,0:T(1,128)S(1)}, f32[1,1,128]{2,1,0:T(1,128)S(1)}, u32[]{:S(2)}, u32[]{:S(2)}) collective-permute-start(f32[1,1,128]{2,1,0:T(1,128)S(1)} %get-tuple-element.36), channel_id=1, source_target_pairs={{1,0},{2,1},{3,2},{5,4},{6,5},{7,6},{9,8},{10,9},{11,10},{13,12},{... | collective-permute-start | bytes 1544 | tf_op jit(solution)/shard_map/ppermute | solution.py:31
  364.0 7.7 %collective-permute-start.23 = (f32[1,1,128]{2,1,0:T(1,128)S(1)}, f32[1,1,128]{2,1,0:T(1,128)S(1)}, u32[]{:S(2)}, u32[]{:S(2)}) collective-permute-start(f32[1,1,128]{2,1,0:T(1,128)S(1)} %get-tuple-element.37), channel_id=1, source_target_pairs={{0,1},{1,2},{2,3},{4,5},{5,6},{6,7},{8,9},{9,10},{10,11},{12,13},{... | collective-permute-start | bytes 1544 | tf_op jit(solution)/shard_map/ppermute | solution.py:28
where the time goes:
time: 485 us; the launch traced here: 484 us
  blocking collectives  323 us (67%)
  starting transfers between devices  134 us (28%)
  between operations  7.24 us (1%)
  other arithmetic  7.13 us (1%)
  waiting for transfers between devices  6.53 us (1%)
  local copies, waits for them, and re-layouts  5.71 us (1%)
    psum x3, blocking collectives, global_total(): return lax.psum(summand, ('tile', 'col'))  323 us
    ppermute x8, starting transfers between devices, padded(): lax.ppermute(lax.slice_in_dim(block, 0, width, axis=dim), axis, backward)  53.6 us
    ppermute x8, starting transfers between devices, partner(): return lax.ppermute(value, axis, pairs)  40.9 us
    ppermute x8, starting transfers between devices, padded(): lax.ppermute(lax.slice_in_dim(block, block.shape[dim] - width, None, axis...  39.8 us
  transfers between devices with their start and end apart: 24, of which 9 were waited for; matrix products, arithmetic and copies ran while one was open for 0% of the time, Pallas kernels for 0%

commit v1 on v0

v1 whole, which is shorter than its diff:
```python
import functools
import math

import jax
import jax.numpy as jnp
from jax import lax
from jax.experimental import pallas as pl
from jax.experimental.pallas import tpu as pltpu
from jax.sharding import PartitionSpec as P

MESH = pl.DeviceIdType.MESH

K = 6
ROWS = 32
COLS = 128
HALO = 8
EXT_ROWS = ROWS + 2 * HALO
EXT_COLS = 2 * COLS

TRACER, U, V, COT, DEPTH, DIAG = 0, K, 2 * K, 3 * K, 4 * K, 4 * K + 1
PLANES = 4 * K + 2
WIDTHS = [6] * K + [5] * K + [4] * K + [4] * K + [6, 1]
OFFSETS = [sum(WIDTHS[:i]) for i in range(PLANES)]

RELAX_MEAN, RELAX_SWING, DAY_STEPS = 0.5, 0.8, 24.0


def shift_x(value, by):
    return pltpu.roll(value, (-by) % value.shape[1], axis=1)


def shift_y(value, by):
    return pltpu.roll(value, (-by) % value.shape[0], axis=0)


def reversed_rows(block):
    row = lax.broadcasted_iota(jnp.int32, (8, block.shape[1]), 0)
    tiles = []
    for start in range(block.shape[0] - 8, -1, -8):
        tile = pltpu.roll(block[start : start + 8], 4, axis=0)
        tile = jnp.where(row % 4 < 2, pltpu.roll(tile, 6, axis=0), pltpu.roll(tile, 2, axis=0))
        tile = jnp.where(row % 2 < 1, pltpu.roll(tile, 7, axis=0), pltpu.roll(tile, 1, axis=0))
        tiles.append(tile)
    return jnp.concatenate(tiles, axis=0)


def groups(tile, col, sizes):
    size_x, size_z, size_y_lo = sizes
    x, z, y_lo = tile % size_x, (tile // size_x) % size_z, tile // (size_x * size_z)
    y, core = (col // 2) * size_y_lo + y_lo, col % 2
    size_y = 2 * size_y_lo

    def device(x, y, z, core):
        return (((y % size_y_lo) * size_z + z) * size_x + x, (y // size_y_lo) * 2 + core)

    chips = []
    for apart in range(1, 2 * size_x):
        place = (x * 2 + core + apart) % (2 * size_x)
        chips.append(device(place // 2, y, z, place % 2))
    alongs_y = [device(x, (y + apart) % size_y, z, core) for apart in range(1, size_y)]
    alongs_z = [device(x, y, (z + apart) % size_z, core) for apart in range(1, size_z)]
    return chips, alongs_y, alongs_z


def kernel(
    sizes,
    tracer_hbm,
    u_hbm,
    v_hbm,
    depth_hbm,
    cot_hbm,
    diag_hbm,
    flip_hbm,
    step_hbm,
    adj_hbm,
    pressure_hbm,
    ext,
    depth_int,
    flips,
    step,
    packed,
    plain,
    mirror,
    mixed,
    raw,
    adj,
    pressure,
    part0,
    part1,
    part2,
    sum0,
    sum1,
    sum2,
    load_sem,
    small_sem,
    store_sem,
    send_sem,
    recv_sem,
    part_send,
    part_recv,
):
    tiles = sizes[0] * sizes[1] * sizes[2]
    tile, col = lax.axis_index("tile"), lax.axis_index("col")
    east, west = (tile + 1) % tiles, (tile + tiles - 1) % tiles
    phases = groups(tile, col, sizes)

    barrier = pltpu.get_barrier_semaphore()
    peers = [(side, other) for side in (east, west) for other in range(4)]
    peers += [(tile, (col + 1) % 4), (tile, (col + 3) % 4)]
    for phase in phases:
        peers += phase
    for peer in peers:
        pl.semaphore_signal(barrier, inc=1, device_id=peer, device_id_type=MESH)

    inner = pl.ds(HALO, ROWS)
    loads = [
        pltpu.make_async_copy(src.at[0], ext.at[pl.ds(plane, K), inner, pl.ds(0, COLS)], load_sem.at[i])
        for i, (src, plane) in enumerate(((tracer_hbm, TRACER), (u_hbm, U), (v_hbm, V), (cot_hbm, COT)))
    ]
    loads.append(pltpu.make_async_copy(diag_hbm.at[0], ext.at[DIAG, inner, pl.ds(0, COLS)], load_sem.at[4]))
    loads.append(pltpu.make_async_copy(depth_hbm.at[0], depth_int, load_sem.at[5]))
    smalls = [
        pltpu.make_async_copy(flip_hbm, flips, small_sem.at[0]),
        pltpu.make_async_copy(step_hbm, step, small_sem.at[1]),
    ]
    for copy in loads + smalls:
        copy.start()
    for copy in loads:
        copy.wait()
    ext[DEPTH, HALO : HALO + ROWS, 0:COLS] = depth_int[...].astype(jnp.float32)

    lane = lax.broadcasted_iota(jnp.int32, (ROWS, COLS), 1)
    for side in range(2):
        block = jnp.zeros((ROWS, COLS), jnp.float32)
        for plane in range(PLANES):
            width, offset = WIDTHS[plane], OFFSETS[plane]
            own = ext[plane, HALO : HALO + ROWS, 0:COLS]
            moved = pltpu.roll(own, (offset + width if side == 0 else offset) % COLS, axis=1)
            block = jnp.where(lane >= offset, moved, block)
        packed[side] = block

    pl.semaphore_wait(barrier, len(peers))

    first, last, whole = pl.ds(0, HALO), pl.ds(ROWS - HALO, HALO), pl.ds(0, ROWS)
    below, above = pl.ds(0, HALO), pl.ds(HALO + ROWS, HALO)
    sends = []

    def seam_copy(side, kind, source, target_block, target, target_col):
        index = side * 6 + kind
        return pltpu.make_async_remote_copy(
            src_ref=packed.at[side, source],
            dst_ref=target_block.at[side, target],
            send_sem=send_sem.at[index],
            recv_sem=recv_sem.at[index],
            device_id=(east if side == 0 else west, target_col),
            device_id_type=MESH,
        )

    def row_copy(index, source, target, target_col):
        return pltpu.make_async_remote_copy(
            src_ref=ext.at[:, source, pl.ds(0, COLS)],
            dst_ref=ext.at[:, target, pl.ds(0, COLS)],
            send_sem=send_sem.at[index],
            recv_sem=recv_sem.at[index],
            device_id=(tile, target_col),
            device_id_type=MESH,
        )

    low, high = col > 0, col < 3
    sends.append((row_copy(12, pl.ds(ROWS, HALO), below, (col + 1) % 4), high, low))
    sends.append((row_copy(13, pl.ds(HALO, HALO), above, (col + 3) % 4), low, high))
    for side in range(2):
        sends.append((seam_copy(side, 3, whole, mirror, inner, 3 - col), None, None))
        sends.append((seam_copy(side, 4, last, mirror, below, (6 - col) % 4), high, high))
        sends.append((seam_copy(side, 5, first, mirror, above, (4 - col) % 4), low, low))
        sends.append((seam_copy(side, 0, whole, plain, inner, col), None, None))
        sends.append((seam_copy(side, 1, last, plain, below, (col + 1) % 4), high, low))
        sends.append((seam_copy(side, 2, first, plain, above, (col + 3) % 4), low, high))

    def maybe(condition, act):
        if condition is None:
            act()
        else:
            pl.when(condition)(act)

    for copy, sending, _ in sends:
        maybe(sending, copy.start)

    for copy in smalls:
        copy.wait()
    flip_east = flips[tile] == 1
    flip_west = flips[west] == 1
    angle = jnp.full((8, COLS), step[0], jnp.int32).astype(jnp.float32) * (2.0 * math.pi / DAY_STEPS)
    kept = 1.0 - (RELAX_MEAN * (1.0 + RELAX_SWING * jnp.cos(angle)))[0:1, 0:1]

    for copy, _, receiving in sends:
        maybe(receiving, copy.wait_recv)

    lane = lax.broadcasted_iota(jnp.int32, (EXT_ROWS, COLS), 1)
    speeds = (lane >= OFFSETS[V]) & (lane < OFFSETS[V + K])

    def beyond_seam(side, flip):
        turned = reversed_rows(mirror[side])
        turned = jnp.where(speeds, -shift_y(turned, 1), turned)
        return jnp.where(flip, turned, plain[side])

    from_west = beyond_seam(0, flip_west)
    from_east = beyond_seam(1, flip_east)
    for plane in range(PLANES):
        width, offset = WIDTHS[plane], OFFSETS[plane]
        right = pltpu.roll(from_east, (COLS - offset) % COLS, axis=1)
        left = pltpu.roll(from_west, (COLS - width - offset) % COLS, axis=1)
        if plane == DEPTH:
            beside = jnp.where(lane < width, right, jnp.where(lane >= COLS - width, left, 0.0))
        else:
            beside = jnp.where(lane < COLS // 2, right, left)
        ext[plane, :, COLS:EXT_COLS] = beside

    row = lax.broadcasted_iota(jnp.int32, (EXT_ROWS, EXT_COLS), 0) + (col * ROWS - HALO)
    inside = (row >= 0) & (row < 4 * ROWS)
    depth = jnp.where(inside, ext[DEPTH], 0.0)
    open_x = jnp.minimum(depth, shift_x(depth, 1))
    open_y = jnp.minimum(depth, shift_y(depth, 1))

    def gated(levels, level, value):
        return jnp.where(levels > float(level), value, 0.0)

    for k in range(K):
        masked = gated(depth, k, ext[TRACER + k])
        change = None
        for shift, levels, speed in ((shift_x, open_x, U), (shift_y, open_y, V)):
            front = shift(masked, 1)
            flux = ext[speed + k] * (
                (7.0 / 12.0) * (masked + front) - (1.0 / 12.0) * (shift(masked, -1) + shift(masked, 2))
            )
            flux = gated(levels, k, flux - 0.4 * (front - masked))
            flux = flux - shift(flux, -1)
            change = flux if change is None else change + flux
        mixed[k] = gated(depth, k, masked - 0.2 * change)

    carry = None
    for k in range(K):
        weight = gated(depth, k, ext[COT + k])
        total = weight * kept if k == 0 else weight
        if carry is not None:
            total = total + carry
        if k + 1 < K:
            gap = mixed[k + 1] - mixed[k]
            bend = jnp.tanh(2.0 * gap)
            slope = 0.6 + 0.5 * bend + gap * (1.0 - bend * bend)
            carry = 0.3 * (weight - gated(depth, k + 1, ext[COT + k + 1])) * gated(depth, k + 1, slope)
            total = total - carry
        raw[k] = gated(depth, k, total)

    rhs = None
    for k in range(K):
        weight = raw[k]
        total = weight
        for shift, levels, speed in ((shift_x, open_x, U), (shift_y, open_y, V)):
            scaled = gated(levels, k, 0.2 * (shift(weight, 1) - weight))
            carried = gated(levels, k, ext[speed + k] * (1.0 / 12.0)) * scaled
            seven, rest = 7.0 * carried, 0.4 * scaled
            total = total + (seven + rest - shift(carried, 1))
            total = total + shift(seven - rest - shift(carried, -1), -1)
        total = gated(depth, k, total)
        adj[k] = total[HALO : HALO + ROWS, 0:COLS]
        rhs = total if rhs is None else rhs + total
    store_adj = pltpu.make_async_copy(adj, adj_hbm.at[0], store_sem.at[0])
    store_adj.start()

    diagonal = jnp.where(inside, ext[DIAG], 0.0)

    def applied(field):
        across = gated(open_x, 0, field - shift_x(field, 1))
        along = gated(open_y, 0, field - shift_y(field, 1))
        return diagonal * field + (across - shift_x(across, -1)) + (along - shift_y(along, -1))

    once = applied(rhs)
    twice = applied(once)[HALO : HALO + ROWS, 0:COLS]
    once = once[HALO : HALO + ROWS, 0:COLS]
    rhs = rhs[HALO : HALO + ROWS, 0:COLS]
    lane = lax.broadcasted_iota(jnp.int32, (1, COLS), 1)
    partial = jnp.zeros((1, COLS), jnp.float32)
    for place, product in enumerate((rhs * rhs, rhs * once, once * once, rhs * twice, once * twice)):
        value = jnp.sum(jnp.sum(product, axis=0, keepdims=True), axis=1, keepdims=True)
        partial = jnp.where(lane == place, value, partial)

    begun = []
    for i, (phase, part, sums) in enumerate(zip(phases, (part0, part1, part2), (sum0, sum1, sum2))):
        part[...] = partial
        for slot, peer in enumerate(phase):
            copy = pltpu.make_async_remote_copy(
                src_ref=part,
                dst_ref=sums.at[slot],
                send_sem=part_send.at[i],
                recv_sem=part_recv.at[i],
                device_id=peer,
                device_id_type=MESH,
            )
            copy.start()
        begun.append(pltpu.make_async_copy(sums, sums, part_send.at[i]))
        pltpu.make_async_copy(sums, sums, part_recv.at[i]).wait()
        for slot in range(len(phase)):
            partial = partial + sums[slot]

    def scalar(place):
        return jnp.sum(jnp.where(lane == place, partial, 0.0), axis=1, keepdims=True)

    g00, g01, g11, g02, g12 = [scalar(place) for place in range(5)]
    step0 = g00 / g01
    norm1 = g00 - 2.0 * step0 * g01 + step0 * step0 * g11
    lift = 1.0 + norm1 / g00
    step1 = norm1 / (
        lift * (lift * g01 - step0 * g02) - step0 * (lift * g11 - step0 * g12)
    )
    pressure[...] = (step0 + step1 * lift) * rhs - (step1 * step0) * once
    store_pressure = pltpu.make_async_copy(pressure, pressure_hbm.at[0], store_sem.at[1])
    store_pressure.start()

    for copy, sending, _ in sends:
        maybe(sending, copy.wait_send)
    for copy in begun:
        copy.wait()
    store_adj.wait()
    store_pressure.wait()


def solution(mesh):
    sizes = (4, 12, 4)
    any_space = pl.BlockSpec(memory_space=pl.ANY)

    def step(tracer_old, u_face, v_face, depth_levels, cotangent, surface_diag, seam_flip, step_index):
        return pl.pallas_call(
            functools.partial(kernel, sizes),
            out_shape=(
                jax.ShapeDtypeStruct(tracer_old.shape, jnp.float32),
                jax.ShapeDtypeStruct(surface_diag.shape, jnp.float32),
            ),
            in_specs=[any_space] * 8,
            out_specs=(any_space, any_space),
            scratch_shapes=[
                pltpu.VMEM((PLANES, EXT_ROWS, EXT_COLS), jnp.float32),
                pltpu.VMEM((ROWS, COLS), jnp.int32),
                pltpu.SMEM(seam_flip.shape, jnp.int32),
                pltpu.SMEM(step_index.shape, jnp.int32),
                pltpu.VMEM((2, ROWS, COLS), jnp.float32),
                pltpu.VMEM((2, EXT_ROWS, COLS), jnp.float32),
                pltpu.VMEM((2, EXT_ROWS, COLS), jnp.float32),
                pltpu.VMEM((K, EXT_ROWS, EXT_COLS), jnp.float32),
                pltpu.VMEM((K, EXT_ROWS, EXT_COLS), jnp.float32),
                pltpu.VMEM((K, ROWS, COLS), jnp.float32),
                pltpu.VMEM((ROWS, COLS), jnp.float32),
                pltpu.VMEM((1, COLS), jnp.float32),
                pltpu.VMEM((1, COLS), jnp.float32),
                pltpu.VMEM((1, COLS), jnp.float32),
                pltpu.VMEM((7, 1, COLS), jnp.float32),
                pltpu.VMEM((7, 1, COLS), jnp.float32),
                pltpu.VMEM((11, 1, COLS), jnp.float32),
                pltpu.SemaphoreType.DMA((6,)),
                pltpu.SemaphoreType.DMA((2,)),
                pltpu.SemaphoreType.DMA((2,)),
                pltpu.SemaphoreType.DMA((14,)),
                pltpu.SemaphoreType.DMA((14,)),
                pltpu.SemaphoreType.DMA((3,)),
                pltpu.SemaphoreType.DMA((3,)),
            ],
            compiler_params=pltpu.CompilerParams(
                collective_id=0, has_side_effects=True, vmem_limit_bytes=32 << 20
            ),
        )(tracer_old, u_face, v_face, depth_levels, cotangent, surface_diag, seam_flip, step_index)

    in_specs = (
        P("tile", None, "col", None),
        P("tile", None, "col", None),
        P("tile", None, "col", None),
        P("tile", "col", None),
        P("tile", None, "col", None),
        P("tile", "col", None),
        P(),
        P(),
    )
    out_specs = (P("tile", None, "col", None), P("tile", "col", None))
    return jax.shard_map(step, mesh=mesh, in_specs=in_specs, out_specs=out_specs, check_vma=False)
```

time: 485 us -> 51 us (0.11)
  blocking collectives: 323 us -> 0 us
  starting transfers between devices: 134 us -> 0 us
  Pallas kernels: 0 us -> 42.8 us
  other arithmetic: 7.13 us -> 0 us
  waiting for transfers between devices: 6.53 us -> 0 us
  between operations: 7.24 us -> 1.32 us
    psum x3 -> x0, blocking collectives: 323 us -> none  [global_total(): return lax.psum(summand, ('tile', 'col'))]
    ppermute x24 -> x0, starting transfers between devices: 134 us -> none  [the longest x8 53.6 us: padded(): lax.ppermute(lax.slice_in_dim(block, 0, width, axis=dim), axis, backward)]
    pallas_call x0 -> x1, Pallas kernels: none -> 42.8 us  [step(): pl.pallas_call(functools.partial(kernel, sizes), out_shape=(jax.ShapeDtyp...]
    ppermute x24 -> x0, waiting for transfers between devices: 6.53 us -> none  [the longest x8 4.72 us: partner(): return lax.ppermute(value, axis, pairs)]
  transfers between devices with their start and end apart: 24 -> 0, of which waited for: 9 -> 0; matrix products, arithmetic and copies ran while one was open for 0% -> 0% of each run, Pallas kernels for 0% -> 0%
where the time goes in v1:
time: 51 us; the launch traced here: 50.3 us
  Pallas kernels  42.8 us (84%)
  local copies, waits for them, and re-layouts  6.26 us (12%)
  between operations  1.32 us (3%)
    pallas_call x1, Pallas kernels, step(): pl.pallas_call(functools.partial(kernel, sizes), out_shape=(jax.ShapeDtyp...  42.8 us
    unnamed x16, local copies, waits for them, and re-layouts  6.26 us

profile of v1, /device:TPU:1, one launch (start us, length us, event | category | flops | bytes accessed | tf_op | source)
XLA Modules:
  0.0 50.3 jit_solution(7937079378313678566)
XLA Ops:
  0.6 0.0 copy-start.6
  1.3 0.0 copy-done.6
  1.3 0.0 copy-start
  1.3 0.9 %copy-done = f32[1,6,32,128]{3,2,1,0:T(8,128)S(1)} copy-done((f32[1,6,32,128]{3,2,1,0:T(8,128)S(1)}, f32[1,6,32,128]{3,2,1,0:T(8,128)}, u32[]{:S(2)}) %copy-start) | copy-done | bytes 98328
  2.2 0.0 copy-start.1
  2.2 0.9 %copy-done.1 = f32[1,6,32,128]{3,2,1,0:T(8,128)S(1)} copy-done((f32[1,6,32,128]{3,2,1,0:T(8,128)S(1)}, f32[1,6,32,128]{3,2,1,0:T(8,128)}, u32[]{:S(2)}) %copy-start.1) | copy-done | bytes 98328
  3.1 0.0 copy-start.2
  3.1 0.9 %copy-done.2 = f32[1,6,32,128]{3,2,1,0:T(8,128)S(1)} copy-done((f32[1,6,32,128]{3,2,1,0:T(8,128)S(1)}, f32[1,6,32,128]{3,2,1,0:T(8,128)}, u32[]{:S(2)}) %copy-start.2) | copy-done | bytes 98328
  4.0 0.0 copy-start.3
  4.0 0.9 %copy-done.3 = f32[1,6,32,128]{3,2,1,0:T(8,128)S(1)} copy-done((f32[1,6,32,128]{3,2,1,0:T(8,128)S(1)}, f32[1,6,32,128]{3,2,1,0:T(8,128)}, u32[]{:S(2)}) %copy-start.3) | copy-done | bytes 98328
  4.9 0.0 copy-start.4
  4.9 0.7 %copy-done.4 = s32[1,32,128]{2,1,0:T(8,128)S(1)} copy-done((s32[1,32,128]{2,1,0:T(8,128)S(1)}, s32[1,32,128]{2,1,0:T(8,128)}, u32[]{:S(2)}) %copy-start.4) | copy-done | bytes 16408
  5.6 0.0 copy-start.5
  5.6 0.7 %copy-done.5 = f32[1,32,128]{2,1,0:T(8,128)S(1)} copy-done((f32[1,32,128]{2,1,0:T(8,128)S(1)}, f32[1,32,128]{2,1,0:T(8,128)}, u32[]{:S(2)}) %copy-start.5) | copy-done | bytes 16408
  6.3 42.8 %shard_map.95 = (f32[1,6,32,128]{3,2,1,0:T(8,128)S(1)}, f32[1,32,128]{2,1,0:T(8,128)S(1)}) custom-call(f32[1,6,32,128]{3,2,1,0:T(8,128)S(1)} %copy-done, f32[1,6,32,128]{3,2,1,0:T(8,128)S(1)} %copy-done.1, f32[1,6,32,128]{3,2,1,0:T(8,128)S(1)} %copy-done.2, s32[1,32,128]{2,1,0:T(8,128)S(1)} %copy-done.4, f32[1,6,32,128]{3,2,1,0:T(8,128)S(1)} %copy-done.3, ...), custom_call_target="tpu_custom_call" | custom-call | tf_op jit(solution)/shard_map/pallas_call | solution.py:333
  49.1 0.6 %copy.13 = f32[1,6,32,128]{3,2,1,0:T(8,128)} copy(f32[1,6,32,128]{3,2,1,0:T(8,128)S(1)} %get-tuple-element.4) | data formatting | bytes 196608
  49.7 0.6 %copy.14 = f32[1,32,128]{2,1,0:T(8,128)} copy(f32[1,32,128]{2,1,0:T(8,128)S(1)} %get-tuple-element.5) | data formatting | bytes 32768
Async XLA Ops:
  0.6 0.7 %copy-start.6 = (s32[192]{0:T(256)S(1)}, s32[192]{0:T(256)}, u32[]{:S(2)}) copy-start(s32[192]{0:T(256)} %flip_hbm.1) | copy-start | bytes 2308
  1.3 0.9 %copy-start = (f32[1,6,32,128]{3,2,1,0:T(8,128)S(1)}, f32[1,6,32,128]{3,2,1,0:T(8,128)}, u32[]{:S(2)}) copy-start(f32[1,6,32,128]{3,2,1,0:T(8,128)} %tracer_hbm.1) | copy-start | bytes 294916
  2.2 0.9 %copy-start.1 = (f32[1,6,32,128]{3,2,1,0:T(8,128)S(1)}, f32[1,6,32,128]{3,2,1,0:T(8,128)}, u32[]{:S(2)}) copy-start(f32[1,6,32,128]{3,2,1,0:T(8,128)} %u_hbm.1) | copy-start | bytes 294916
  3.1 0.9 %copy-start.2 = (f32[1,6,32,128]{3,2,1,0:T(8,128)S(1)}, f32[1,6,32,128]{3,2,1,0:T(8,128)}, u32[]{:S(2)}) copy-start(f32[1,6,32,128]{3,2,1,0:T(8,128)} %v_hbm.1) | copy-start | bytes 294916
  4.0 0.9 %copy-start.3 = (f32[1,6,32,128]{3,2,1,0:T(8,128)S(1)}, f32[1,6,32,128]{3,2,1,0:T(8,128)}, u32[]{:S(2)}) copy-start(f32[1,6,32,128]{3,2,1,0:T(8,128)} %cot_hbm.1) | copy-start | bytes 294916
  4.9 0.7 %copy-start.4 = (s32[1,32,128]{2,1,0:T(8,128)S(1)}, s32[1,32,128]{2,1,0:T(8,128)}, u32[]{:S(2)}) copy-start(s32[1,32,128]{2,1,0:T(8,128)} %depth_hbm.1) | copy-start | bytes 49156
  5.6 0.7 %copy-start.5 = (f32[1,32,128]{2,1,0:T(8,128)S(1)}, f32[1,32,128]{2,1,0:T(8,128)}, u32[]{:S(2)}) copy-start(f32[1,32,128]{2,1,0:T(8,128)} %diag_hbm.1) | copy-start | bytes 49156

commit v2 on v1

--- a/solution.py
+++ b/solution.py
@@ -46,20 +46,33 @@
 
 def groups(tile, col, sizes):
     size_x, size_z, size_y_lo = sizes
-    x, z, y_lo = tile % size_x, (tile // size_x) % size_z, tile // (size_x * size_z)
-    y, core = (col // 2) * size_y_lo + y_lo, col % 2
+    x, z = lax.rem(tile, size_x), lax.rem(lax.div(tile, size_x), size_z)
+    y_lo = lax.div(tile, size_x * size_z)
+    y_hi, core = lax.div(col, 2), lax.rem(col, 2)
+    y = y_hi * size_y_lo + y_lo
     size_y = 2 * size_y_lo
 
     def device(x, y, z, core):
-        return (((y % size_y_lo) * size_z + z) * size_x + x, (y // size_y_lo) * 2 + core)
-
-    chips = []
-    for apart in range(1, 2 * size_x):
-        place = (x * 2 + core + apart) % (2 * size_x)
-        chips.append(device(place // 2, y, z, place % 2))
-    alongs_y = [device(x, (y + apart) % size_y, z, core) for apart in range(1, size_y)]
-    alongs_z = [device(x, y, (z + apart) % size_z, core) for apart in range(1, size_z)]
-    return chips, alongs_y, alongs_z
+        y_hi = lax.div(y, size_y_lo)
+        y_lo = y - y_hi * size_y_lo
+        return ((y_lo * size_z + z) * size_x + x, y_hi * 2 + core)
+
+    def farthest_first(count):
+        return sorted(range(1, count), key=lambda apart: -min(apart, count - apart))
+
+    columns = []
+    for apart in farthest_first(2 * size_z):
+        place = lax.rem(z * 2 + core + apart, 2 * size_z)
+        columns.append(device(x, y, lax.div(place, 2), lax.rem(place, 2)))
+    xs = [lax.rem(x + apart, size_x) for apart in range(size_x)]
+    ys = [lax.rem(y + apart, size_y) for apart in range(size_y)]
+    planes = []
+    for apart in sorted(
+        range(1, size_x * size_y),
+        key=lambda a: -min(a % size_x, size_x - a % size_x) - min(a // size_x, size_y - a // size_x),
+    ):
+        planes.append(device(xs[apart % size_x], ys[apart // size_x], z, core))
+    return columns, planes
 
 
 def kernel(
@@ -72,28 +85,25 @@
     diag_hbm,
     flip_hbm,
     step_hbm,
-    adj_hbm,
-    pressure_hbm,
+    adj_out,
+    pressure_out,
     ext,
     depth_int,
     flips,
     step,
     packed,
+    rows_out,
+    rows_in,
     plain,
     mirror,
     mixed,
     raw,
-    adj,
-    pressure,
     part0,
     part1,
-    part2,
     sum0,
     sum1,
-    sum2,
     load_sem,
     small_sem,
-    store_sem,
     send_sem,
     recv_sem,
     part_send,
@@ -101,17 +111,14 @@
 ):
     tiles = sizes[0] * sizes[1] * sizes[2]
     tile, col = lax.axis_index("tile"), lax.axis_index("col")
-    east, west = (tile + 1) % tiles, (tile + tiles - 1) % tiles
+    east, west = lax.rem(tile + 1, tiles), lax.rem(tile + tiles - 1, tiles)
     phases = groups(tile, col, sizes)
 
     barrier = pltpu.get_barrier_semaphore()
     peers = [(side, other) for side in (east, west) for other in range(4)]
-    peers += [(tile, (col + 1) % 4), (tile, (col + 3) % 4)]
+    peers += [(tile, lax.rem(col + 1, 4)), (tile, lax.rem(col + 3, 4))]
     for phase in phases:
         peers += phase
-    for peer in peers:
-        pl.semaphore_signal(barrier, inc=1, device_id=peer, device_id_type=MESH)
-
     inner = pl.ds(HALO, ROWS)
     loads = [
         pltpu.make_async_copy(src.at[0], ext.at[pl.ds(plane, K), inner, pl.ds(0, COLS)], load_sem.at[i])
@@ -125,6 +132,9 @@
     ]
     for copy in loads + smalls:
         copy.start()
+    for peer in peers:
+        pl.semaphore_signal(barrier, inc=1, device_id=peer, device_id_type=MESH)
+
     for copy in loads:
         copy.wait()
     ext[DEPTH, HALO : HALO + ROWS, 0:COLS] = depth_int[...].astype(jnp.float32)
@@ -138,6 +148,29 @@
             moved = pltpu.roll(own, (offset + width if side == 0 else offset) % COLS, axis=1)
             block = jnp.where(lane >= offset, moved, block)
         packed[side] = block
+
+    spot = lax.broadcasted_iota(jnp.int32, (HALO, COLS), 0)
+
+    def end_tile(plane, way):
+        start = ROWS if way == 0 else HALO
+        return ext[plane, start : start + HALO, 0:COLS]
+
+    for way in range(2):
+        half = (spot >= 4) if way == 0 else (spot < 4)
+        six = (spot >= 2) if way == 0 else (spot < 6)
+        for k in range(K):
+            tracer_tile, v_tile = end_tile(TRACER + k, way), end_tile(V + k, way)
+            if way == 0:
+                tracer_tile = jnp.where(six, tracer_tile, pltpu.roll(v_tile, 6, axis=0))
+            rows_out[way, k] = tracer_tile
+            rows_out[way, K + k] = jnp.where(
+                half, end_tile(U + k, way), pltpu.roll(end_tile(COT + k, way), 4, axis=0)
+            )
+            if k % 2 == 0:
+                other = pltpu.roll(end_tile(V + k + 1, way), 4, axis=0)
+                rows_out[way, 2 * K + k // 2] = jnp.where(half, v_tile, other)
+        diagonal_tile = pltpu.roll(end_tile(DIAG, way), 1 if way == 0 else 7, axis=0)
+        rows_out[way, 2 * K + K // 2] = jnp.where(six, end_tile(DEPTH, way), diagonal_tile)
 
     pl.semaphore_wait(barrier, len(peers))
 
@@ -156,10 +189,10 @@
             device_id_type=MESH,
         )
 
-    def row_copy(index, source, target, target_col):
+    def row_copy(index, way, target_col):
         return pltpu.make_async_remote_copy(
-            src_ref=ext.at[:, source, pl.ds(0, COLS)],
-            dst_ref=ext.at[:, target, pl.ds(0, COLS)],
+            src_ref=rows_out.at[way],
+            dst_ref=rows_in.at[way],
             send_sem=send_sem.at[index],
             recv_sem=recv_sem.at[index],
             device_id=(tile, target_col),
@@ -167,15 +200,15 @@
         )
 
     low, high = col > 0, col < 3
-    sends.append((row_copy(12, pl.ds(ROWS, HALO), below, (col + 1) % 4), high, low))
-    sends.append((row_copy(13, pl.ds(HALO, HALO), above, (col + 3) % 4), low, high))
     for side in range(2):
         sends.append((seam_copy(side, 3, whole, mirror, inner, 3 - col), None, None))
-        sends.append((seam_copy(side, 4, last, mirror, below, (6 - col) % 4), high, high))
-        sends.append((seam_copy(side, 5, first, mirror, above, (4 - col) % 4), low, low))
+        sends.append((seam_copy(side, 4, last, mirror, below, lax.rem(6 - col, 4)), high, high))
+        sends.append((seam_copy(side, 5, first, mirror, above, lax.rem(4 - col, 4)), low, low))
         sends.append((seam_copy(side, 0, whole, plain, inner, col), None, None))
-        sends.append((seam_copy(side, 1, last, plain, below, (col + 1) % 4), high, low))
-        sends.append((seam_copy(side, 2, first, plain, above, (col + 3) % 4), low, high))
+        sends.append((seam_copy(side, 1, last, plain, below, lax.rem(col + 1, 4)), high, low))
+        sends.append((seam_copy(side, 2, first, plain, above, lax.rem(col + 3, 4)), low, high))
+    sends.append((row_copy(12, 0, lax.rem(col + 1, 4)), high, low))
+    sends.append((row_copy(13, 1, lax.rem(col + 3, 4)), low, high))
 
     def maybe(condition, act):
         if condition is None:
@@ -195,6 +228,28 @@
 
     for copy, _, receiving in sends:
         maybe(receiving, copy.wait_recv)
+
+    for way in range(2):
+        half = (spot >= 4) if way == 0 else (spot < 4)
+        start = 0 if way == 0 else HALO + ROWS
+
+        def put(plane, value):
+            ext[plane, start : start + HALO, 0:COLS] = value
+
+        for k in range(K):
+            tracer_tile, mixed_tile = rows_in[way, k], rows_in[way, K + k]
+            put(TRACER + k, tracer_tile)
+            put(U + k, mixed_tile)
+            put(COT + k, pltpu.roll(mixed_tile, 4, axis=0))
+            v_tile = rows_in[way, 2 * K + k // 2]
+            if k % 2 == 1:
+                v_tile = pltpu.roll(v_tile, 4, axis=0)
+            if way == 0:
+                v_tile = jnp.where(half, v_tile, pltpu.roll(tracer_tile, 2, axis=0))
+            put(V + k, v_tile)
+        depth_tile = rows_in[way, 2 * K + K // 2]
+        put(DEPTH, depth_tile)
+        put(DIAG, pltpu.roll(depth_tile, 7 if way == 0 else 1, axis=0))
 
     lane = lax.broadcasted_iota(jnp.int32, (EXT_ROWS, COLS), 1)
     speeds = (lane >= OFFSETS[V]) & (lane < OFFSETS[V + K])
@@ -218,7 +273,8 @@
 
     row = lax.broadcasted_iota(jnp.int32, (EXT_ROWS, EXT_COLS), 0) + (col * ROWS - HALO)
     inside = (row >= 0) & (row < 4 * ROWS)
-    depth = jnp.where(inside, ext[DEPTH], 0.0)
+    place = row - col * ROWS
+    depth = jnp.where(inside & (place >= -6) & (place < ROWS + 6), ext[DEPTH], 0.0)
     open_x = jnp.minimum(depth, shift_x(depth, 1))
     open_y = jnp.minimum(depth, shift_y(depth, 1))
 
@@ -263,10 +319,8 @@
             total = total + (seven + rest - shift(carried, 1))
             total = total + shift(seven - rest - shift(carried, -1), -1)
         total = gated(depth, k, total)
-        adj[k] = total[HALO : HALO + ROWS, 0:COLS]
+        adj_out[0, k] = total[HALO : HALO + ROWS, 0:COLS]
         rhs = total if rhs is None else rhs + total
-    store_adj = pltpu.make_async_copy(adj, adj_hbm.at[0], store_sem.at[0])
-    store_adj.start()
 
     diagonal = jnp.where(inside, ext[DIAG], 0.0)
 
@@ -286,7 +340,7 @@
         partial = jnp.where(lane == place, value, partial)
 
     begun = []
-    for i, (phase, part, sums) in enumerate(zip(phases, (part0, part1, part2), (sum0, sum1, sum2))):
+    for i, (phase, part, sums) in enumerate(zip(phases, (part0, part1), (sum0, sum1))):
         part[...] = partial
         for slot, peer in enumerate(phase):
             copy = pltpu.make_async_remote_copy(
@@ -313,16 +367,12 @@
     step1 = norm1 / (
         lift * (lift * g01 - step0 * g02) - step0 * (lift * g11 - step0 * g12)
     )
-    pressure[...] = (step0 + step1 * lift) * rhs - (step1 * step0) * once
-    store_pressure = pltpu.make_async_copy(pressure, pressure_hbm.at[0], store_sem.at[1])
-    store_pressure.start()
+    pressure_out[0] = (step0 + step1 * lift) * rhs - (step1 * step0) * once
 
     for copy, sending, _ in sends:
         maybe(sending, copy.wait_send)
     for copy in begun:
         copy.wait()
-    store_adj.wait()
-    store_pressure.wait()
 
 
 def solution(mesh):
@@ -337,35 +387,32 @@
                 jax.ShapeDtypeStruct(surface_diag.shape, jnp.float32),
             ),
             in_specs=[any_space] * 8,
-            out_specs=(any_space, any_space),
+            out_specs=(pl.BlockSpec(memory_space=pltpu.VMEM), pl.BlockSpec(memory_space=pltpu.VMEM)),
             scratch_shapes=[
                 pltpu.VMEM((PLANES, EXT_ROWS, EXT_COLS), jnp.float32),
                 pltpu.VMEM((ROWS, COLS), jnp.int32),
                 pltpu.SMEM(seam_flip.shape, jnp.int32),
                 pltpu.SMEM(step_index.shape, jnp.int32),
                 pltpu.VMEM((2, ROWS, COLS), jnp.float32),
+                pltpu.VMEM((2, 2 * K + K // 2 + 1, HALO, COLS), jnp.float32),
+                pltpu.VMEM((2, 2 * K + K // 2 + 1, HALO, COLS), jnp.float32),
                 pltpu.VMEM((2, EXT_ROWS, COLS), jnp.float32),
                 pltpu.VMEM((2, EXT_ROWS, COLS), jnp.float32),
                 pltpu.VMEM((K, EXT_ROWS, EXT_COLS), jnp.float32),
                 pltpu.VMEM((K, EXT_ROWS, EXT_COLS), jnp.float32),
-                pltpu.VMEM((K, ROWS, COLS), jnp.float32),
-                pltpu.VMEM((ROWS, COLS), jnp.float32),
                 pltpu.VMEM((1, COLS), jnp.float32),
                 pltpu.VMEM((1, COLS), jnp.float32),
-                pltpu.VMEM((1, COLS), jnp.float32),
-                pltpu.VMEM((7, 1, COLS), jnp.float32),
-                pltpu.VMEM((7, 1, COLS), jnp.float32),
-                pltpu.VMEM((11, 1, COLS), jnp.float32),
+                pltpu.VMEM((23, 1, COLS), jnp.float32),
+                pltpu.VMEM((31, 1, COLS), jnp.float32),
                 pltpu.SemaphoreType.DMA((6,)),
-                pltpu.SemaphoreType.DMA((2,)),
                 pltpu.SemaphoreType.DMA((2,)),
                 pltpu.SemaphoreType.DMA((14,)),
                 pltpu.SemaphoreType.DMA((14,)),
-                pltpu.SemaphoreType.DMA((3,)),
-                pltpu.SemaphoreType.DMA((3,)),
+                pltpu.SemaphoreType.DMA((2,)),
+                pltpu.SemaphoreType.DMA((2,)),
             ],
             compiler_params=pltpu.CompilerParams(
-                collective_id=0, has_side_effects=True, vmem_limit_bytes=32 << 20
+                collective_id=0, has_side_effects=True
             ),
         )(tracer_old, u_face, v_face, depth_levels, cotangent, surface_diag, seam_flip, step_index)
 

time: 51 us -> 44.6 us (0.87)
  local copies, waits for them, and re-layouts: 6.26 us -> 2.15 us
  Pallas kernels: 42.8 us -> 41 us
    unnamed x16 -> x4, local copies, waits for them, and re-layouts: 6.26 us -> 2.15 us
    pallas_call x1, Pallas kernels: 42.8 us -> 41 us  [step(): pl.pallas_call(functools.partial(kernel, sizes), out_shape=(jax.ShapeDtyp...]
where the time goes in v2:
time: 44.6 us; the launch traced here: 44.4 us
  Pallas kernels  41 us (92%)
  local copies, waits for them, and re-layouts  2.15 us (5%)
  between operations  1.3 us (3%)
    pallas_call x1, Pallas kernels, step(): pl.pallas_call(functools.partial(kernel, sizes), out_shape=(jax.ShapeDtyp...  41 us
    unnamed x4, local copies, waits for them, and re-layouts  2.15 us

profile of v2, /device:TPU:1, one launch (start us, length us, event | category | flops | bytes accessed | tf_op | source)
XLA Modules:
  0.0 44.4 jit_solution(13068541005832485274)
XLA Ops:
  1.3 41.0 %shard_map.95 = (f32[1,6,32,128]{3,2,1,0:T(8,128)}, f32[1,32,128]{2,1,0:T(8,128)}) custom-call(f32[1,6,32,128]{3,2,1,0:T(8,128)} %tracer_hbm.1, f32[1,6,32,128]{3,2,1,0:T(8,128)} %u_hbm.1, f32[1,6,32,128]{3,2,1,0:T(8,128)} %v_hbm.1, s32[1,32,128]{2,1,0:T(8,128)} %depth_hbm.1, f32[1,6,32,128]{3,2,1,0:T(8,128)} %cot_hbm.1, f32[1,32,128]{2,1,0:T(8,128)} %diag_hbm.1, ...), custom_call_target="tpu_custom_call" | custom-call | tf_op jit(solution)/shard_map/pallas_call | solution.py:383
  42.3 0.0 copy-start
  42.3 1.5 %copy.13 = f32[1,6,32,128]{3,2,1,0:T(8,128)} copy(f32[1,6,32,128]{3,2,1,0:T(8,128)} %get-tuple-element.4) | data formatting | bytes 196608
  43.8 0.0 copy-done
  43.8 0.6 %copy.14 = f32[1,32,128]{2,1,0:T(8,128)} copy(f32[1,32,128]{2,1,0:T(8,128)S(1)} %copy-done) | data formatting | bytes 32768
Async XLA Ops:
  42.3 1.6 %copy-start = (f32[1,32,128]{2,1,0:T(8,128)S(1)}, f32[1,32,128]{2,1,0:T(8,128)}, u32[]{:S(2)}) copy-start(f32[1,32,128]{2,1,0:T(8,128)} %get-tuple-element.5) | copy-start | bytes 49156

commit v3 on v2

--- a/solution.py
+++ b/solution.py
@@ -85,8 +85,8 @@
     diag_hbm,
     flip_hbm,
     step_hbm,
-    adj_out,
-    pressure_out,
+    adj_hbm,
+    pressure_hbm,
     ext,
     depth_int,
     flips,
@@ -94,6 +94,8 @@
     packed,
     rows_out,
     rows_in,
+    adj_out,
+    pressure_out,
     plain,
     mirror,
     mixed,
@@ -104,6 +106,7 @@
     sum1,
     load_sem,
     small_sem,
+    store_sem,
     send_sem,
     recv_sem,
     part_send,
@@ -319,8 +322,11 @@
             total = total + (seven + rest - shift(carried, 1))
             total = total + shift(seven - rest - shift(carried, -1), -1)
         total = gated(depth, k, total)
-        adj_out[0, k] = total[HALO : HALO + ROWS, 0:COLS]
+        adj_out[k] = total[HALO : HALO + ROWS, 0:COLS]
         rhs = total if rhs is None else rhs + total
+
+    store_adj = pltpu.make_async_copy(adj_out, adj_hbm.at[0], store_sem.at[0])
+    store_adj.start()
 
     diagonal = jnp.where(inside, ext[DIAG], 0.0)
 
@@ -367,12 +373,30 @@
     step1 = norm1 / (
         lift * (lift * g01 - step0 * g02) - step0 * (lift * g11 - step0 * g12)
     )
-    pressure_out[0] = (step0 + step1 * lift) * rhs - (step1 * step0) * once
-
+    pressure_out[...] = (step0 + step1 * lift) * rhs - (step1 * step0) * once
+
+    store_pressure = pltpu.make_async_copy(pressure_out, pressure_hbm.at[0], store_sem.at[1])
+    store_pressure.start()
     for copy, sending, _ in sends:
         maybe(sending, copy.wait_send)
     for copy in begun:
         copy.wait()
+    store_adj.wait()
+    store_pressure.wait()
+
+
+def hand_over(adj_in, pressure_in, adj_out, pressure_out, adj_held, pressure_held, sem):
+    parts = [(pressure_in, pressure_held, pressure_out)]
+    parts += [(adj_in.at[:, h], adj_held.at[:, h], adj_out.at[:, h]) for h in (pl.ds(0, K // 2), pl.ds(K // 2, K // 2))]
+    loads = [pltpu.make_async_copy(a, b, sem.at[0, i]) for i, (a, b, _) in enumerate(parts)]
+    stores = [pltpu.make_async_copy(b, c, sem.at[1, i]) for i, (_, b, c) in enumerate(parts)]
+    for copy in loads:
+        copy.start()
+    for load, store in zip(loads, stores):
+        load.wait()
+        store.start()
+    for copy in stores:
+        copy.wait()
 
 
 def solution(mesh):
@@ -380,14 +404,14 @@
     any_space = pl.BlockSpec(memory_space=pl.ANY)
 
     def step(tracer_old, u_face, v_face, depth_levels, cotangent, surface_diag, seam_flip, step_index):
-        return pl.pallas_call(
+        results = pl.pallas_call(
             functools.partial(kernel, sizes),
             out_shape=(
                 jax.ShapeDtypeStruct(tracer_old.shape, jnp.float32),
                 jax.ShapeDtypeStruct(surface_diag.shape, jnp.float32),
             ),
             in_specs=[any_space] * 8,
-            out_specs=(pl.BlockSpec(memory_space=pltpu.VMEM), pl.BlockSpec(memory_space=pltpu.VMEM)),
+            out_specs=(any_space, any_space),
             scratch_shapes=[
                 pltpu.VMEM((PLANES, EXT_ROWS, EXT_COLS), jnp.float32),
                 pltpu.VMEM((ROWS, COLS), jnp.int32),
@@ -396,6 +420,8 @@
                 pltpu.VMEM((2, ROWS, COLS), jnp.float32),
                 pltpu.VMEM((2, 2 * K + K // 2 + 1, HALO, COLS), jnp.float32),
                 pltpu.VMEM((2, 2 * K + K // 2 + 1, HALO, COLS), jnp.float32),
+                pltpu.VMEM((K, ROWS, COLS), jnp.float32),
+                pltpu.VMEM((ROWS, COLS), jnp.float32),
                 pltpu.VMEM((2, EXT_ROWS, COLS), jnp.float32),
                 pltpu.VMEM((2, EXT_ROWS, COLS), jnp.float32),
                 pltpu.VMEM((K, EXT_ROWS, EXT_COLS), jnp.float32),
@@ -406,6 +432,7 @@
                 pltpu.VMEM((31, 1, COLS), jnp.float32),
                 pltpu.SemaphoreType.DMA((6,)),
                 pltpu.SemaphoreType.DMA((2,)),
+                pltpu.SemaphoreType.DMA((2,)),
                 pltpu.SemaphoreType.DMA((14,)),
                 pltpu.SemaphoreType.DMA((14,)),
                 pltpu.SemaphoreType.DMA((2,)),
@@ -415,6 +442,21 @@
                 collective_id=0, has_side_effects=True
             ),
         )(tracer_old, u_face, v_face, depth_levels, cotangent, surface_diag, seam_flip, step_index)
+
+        return pl.pallas_call(
+            hand_over,
+            out_shape=(
+                jax.ShapeDtypeStruct(tracer_old.shape, jnp.float32),
+                jax.ShapeDtypeStruct(surface_diag.shape, jnp.float32),
+            ),
+            in_specs=[any_space] * 2,
+            out_specs=(any_space, any_space),
+            scratch_shapes=[
+                pltpu.VMEM((1, K, ROWS, COLS), jnp.float32),
+                pltpu.VMEM((1, ROWS, COLS), jnp.float32),
+                pltpu.SemaphoreType.DMA((2, 3)),
+            ],
+        )(*results)
 
     in_specs = (
         P("tile", None, "col", None),

time: 44.6 us -> 44 us (0.987)
  local copies, waits for them, and re-layouts: 2.15 us -> 0 us
  Pallas kernels: 41 us -> 42.4 us
    unnamed x4 -> x0, local copies, waits for them, and re-layouts: 2.15 us -> none
    pallas_call x0 -> x1, Pallas kernels: none -> 1.51 us  [step(): pl.pallas_call(hand_over, out_shape=(jax.ShapeDtypeStruct(tracer_old.shap...]
where the time goes in v3:
time: 44 us; the launch traced here: 43.7 us
  Pallas kernels  42.4 us (96%)
  between operations  1.29 us (3%)
    pallas_call x1, Pallas kernels, step(): pl.pallas_call(functools.partial(kernel, sizes), out_shape=(jax.ShapeDtyp...  40.9 us
    pallas_call x1, Pallas kernels, step(): pl.pallas_call(hand_over, out_shape=(jax.ShapeDtypeStruct(tracer_old.shap...  1.51 us

profile of v3, /device:TPU:1, one launch (start us, length us, event | category | flops | bytes accessed | tf_op | source)
XLA Modules:
  0.0 43.7 jit_solution(7262484696525302938)
XLA Ops:
  1.3 40.9 %shard_map.95 = (f32[1,6,32,128]{3,2,1,0:T(8,128)}, f32[1,32,128]{2,1,0:T(8,128)}) custom-call(f32[1,6,32,128]{3,2,1,0:T(8,128)} %tracer_hbm.1, f32[1,6,32,128]{3,2,1,0:T(8,128)} %u_hbm.1, f32[1,6,32,128]{3,2,1,0:T(8,128)} %v_hbm.1, s32[1,32,128]{2,1,0:T(8,128)} %depth_hbm.1, f32[1,6,32,128]{3,2,1,0:T(8,128)} %cot_hbm.1, f32[1,32,128]{2,1,0:T(8,128)} %diag_hbm.1, ...), custom_call_target="tpu_custom_call" | custom-call | tf_op jit(solution)/shard_map/pallas_call | solution.py:407
  42.2 1.5 %shard_map.96 = (f32[1,6,32,128]{3,2,1,0:T(8,128)}, f32[1,32,128]{2,1,0:T(8,128)}) custom-call(f32[1,6,32,128]{3,2,1,0:T(8,128)} %get-tuple-element.4.adj_in, f32[1,32,128]{2,1,0:T(8,128)} %get-tuple-element.5.pressure_in), custom_call_target="tpu_custom_call" | custom-call | tf_op jit(solution)/shard_map/pallas_call | solution.py:446

commit v4 on v3

--- a/solution.py
+++ b/solution.py
@@ -229,9 +229,33 @@
     angle = jnp.full((8, COLS), step[0], jnp.int32).astype(jnp.float32) * (2.0 * math.pi / DAY_STEPS)
     kept = 1.0 - (RELAX_MEAN * (1.0 + RELAX_SWING * jnp.cos(angle)))[0:1, 0:1]
 
-    for copy, _, receiving in sends:
+    seams, ends = sends[:-2], sends[-2:]
+    for copy, _, receiving in seams:
         maybe(receiving, copy.wait_recv)
 
+
+    lane = lax.broadcasted_iota(jnp.int32, (EXT_ROWS, COLS), 1)
+    speeds = (lane >= OFFSETS[V]) & (lane < OFFSETS[V + K])
+
+    def beyond_seam(side, flip):
+        turned = reversed_rows(mirror[side])
+        turned = jnp.where(speeds, -shift_y(turned, 1), turned)
+        return jnp.where(flip, turned, plain[side])
+
+    from_west = beyond_seam(0, flip_west)
+    from_east = beyond_seam(1, flip_east)
+    for plane in range(PLANES):
+        width, offset = WIDTHS[plane], OFFSETS[plane]
+        right = pltpu.roll(from_east, (COLS - offset) % COLS, axis=1)
+        left = pltpu.roll(from_west, (COLS - width - offset) % COLS, axis=1)
+        if plane == DEPTH:
+            beside = jnp.where(lane < width, right, jnp.where(lane >= COLS - width, left, 0.0))
+        else:
+            beside = jnp.where(lane < COLS // 2, right, left)
+        ext[plane, :, COLS:EXT_COLS] = beside
+
+    for copy, _, receiving in ends:
+        maybe(receiving, copy.wait_recv)
     for way in range(2):
         half = (spot >= 4) if way == 0 else (spot < 4)
         start = 0 if way == 0 else HALO + ROWS
@@ -253,26 +277,6 @@
         depth_tile = rows_in[way, 2 * K + K // 2]
         put(DEPTH, depth_tile)
         put(DIAG, pltpu.roll(depth_tile, 7 if way == 0 else 1, axis=0))
-
-    lane = lax.broadcasted_iota(jnp.int32, (EXT_ROWS, COLS), 1)
-    speeds = (lane >= OFFSETS[V]) & (lane < OFFSETS[V + K])
-
-    def beyond_seam(side, flip):
-        turned = reversed_rows(mirror[side])
-        turned = jnp.where(speeds, -shift_y(turned, 1), turned)
-        return jnp.where(flip, turned, plain[side])
-
-    from_west = beyond_seam(0, flip_west)
-    from_east = beyond_seam(1, flip_east)
-    for plane in range(PLANES):
-        width, offset = WIDTHS[plane], OFFSETS[plane]
-        right = pltpu.roll(from_east, (COLS - offset) % COLS, axis=1)
-        left = pltpu.roll(from_west, (COLS - width - offset) % COLS, axis=1)
-        if plane == DEPTH:
-            beside = jnp.where(lane < width, right, jnp.where(lane >= COLS - width, left, 0.0))
-        else:
-            beside = jnp.where(lane < COLS // 2, right, left)
-        ext[plane, :, COLS:EXT_COLS] = beside
 
     row = lax.broadcasted_iota(jnp.int32, (EXT_ROWS, EXT_COLS), 0) + (col * ROWS - HALO)
     inside = (row >= 0) & (row < 4 * ROWS)

time: 44 us -> 44 us (level)
  no operation moved by 1% of the time
where the time goes in v4:
time: 44 us; the launch traced here: 43.8 us
  Pallas kernels  42.5 us (97%)
  between operations  1.29 us (3%)
    pallas_call x1, Pallas kernels, step(): pl.pallas_call(functools.partial(kernel, sizes), out_shape=(jax.ShapeDtyp...  41 us
    pallas_call x1, Pallas kernels, step(): pl.pallas_call(hand_over, out_shape=(jax.ShapeDtypeStruct(tracer_old.shap...  1.51 us

profile of v4, /device:TPU:1, one launch (start us, length us, event | category | flops | bytes accessed | tf_op | source)
XLA Modules:
  0.0 43.8 jit_solution(9040596172196796354)
XLA Ops:
  1.3 41.0 %shard_map.95 = (f32[1,6,32,128]{3,2,1,0:T(8,128)}, f32[1,32,128]{2,1,0:T(8,128)}) custom-call(f32[1,6,32,128]{3,2,1,0:T(8,128)} %tracer_hbm.1, f32[1,6,32,128]{3,2,1,0:T(8,128)} %u_hbm.1, f32[1,6,32,128]{3,2,1,0:T(8,128)} %v_hbm.1, s32[1,32,128]{2,1,0:T(8,128)} %depth_hbm.1, f32[1,6,32,128]{3,2,1,0:T(8,128)} %cot_hbm.1, f32[1,32,128]{2,1,0:T(8,128)} %diag_hbm.1, ...), custom_call_target="tpu_custom_call" | custom-call | tf_op jit(solution)/shard_map/pallas_call | solution.py:411
  42.3 1.5 %shard_map.96 = (f32[1,6,32,128]{3,2,1,0:T(8,128)}, f32[1,32,128]{2,1,0:T(8,128)}) custom-call(f32[1,6,32,128]{3,2,1,0:T(8,128)} %get-tuple-element.4.adj_in, f32[1,32,128]{2,1,0:T(8,128)} %get-tuple-element.5.pressure_in), custom_call_target="tpu_custom_call" | custom-call | tf_op jit(solution)/shard_map/pallas_call | solution.py:450
